TPU v7x, 32 devices: a whole 2x2x4 slice. The times are simulated.
32 devices in a mesh: streams: 2 (over x), frames: 16 (over z, y, core).
Axes of the slice: x: 2, y: 2, z: 4, core: 2. Of those that a mesh axis runs over, the one named last changes fastest.
Arguments:
- features: bfloat16 [65536, 256], P(('streams', 'frames')), parts along dimension 0, may hold values from -9 to 9
- start_block: bfloat16 [65536, 128], P(('streams', 'frames')), parts along dimension 0, may hold values from -6 to 6
- counts: int32 [128], P(('streams', 'frames')), parts along dimension 0, may hold values from 128 to 512, as said below
- reach: int32 [128], P(('streams', 'frames')), parts along dimension 0, may hold values from 0 to 2, as said below
Outputs:
- basis: float32 [65536, 128], P(('streams', 'frames')), parts along dimension 0
- rayleigh: float32 [256, 128], P('streams'), parts along dimension 0
There are 2 independent parts, one for each index of `streams`. A program takes and returns all parts, laid end to end along the dimension named above; each array names one. Nothing has to cross between parts.
Inputs may be any that keep to these rules, and one draw needn't show every extreme that they name: `counts`: each band block has at least 128 valid frames; some block is full and some has exactly 128. reach[b] never passes the last block of the stream; some block reaches 2 blocks ahead.
All inputs are finite; a program needn't handle non-finite values.
Results may differ from a plain program's by a relative error of at most 0.012.
Values may be sent and summed in bfloat16 or wider, within the bound.
A program may use at most 64 MiB of HBM per device.

v0:
```python
import math

import jax
import jax.numpy as jnp
from jax import lax
from jax.sharding import PartitionSpec as P

BLOCK = 512
MAXREACH = 2
ITERS = 3


def shifted(value, axis, steps):
    count = lax.axis_size(axis)
    initial, last = (max(0, -steps), min(count, count - steps))
    return lax.ppermute(value, axis, [(source, source + steps) for source in range(initial, last)])


def affinity(row_x, row_m, col_x, col_m, gamma):
    row_n = jnp.sum(jnp.square(row_x.astype(jnp.float32)), 1)
    col_n = jnp.sum(jnp.square(col_x.astype(jnp.float32)), 1)
    inner = lax.dot_general(
        row_x, col_x, (((1,), (1,)), ((), ())), preferred_element_type=jnp.float32
    )
    dist = row_n[:, None] + col_n[None, :] - 2.0 * inner
    return jnp.exp(-gamma * dist) * row_m[:, None] * col_m[None, :]


def contribute(row_x, row_m, row_v, col_x, col_m, col_v, gamma, active, with_back):
    tile = affinity(row_x, row_m, col_x, col_m, gamma) * active.astype(jnp.float32)
    tile = tile.astype(jnp.bfloat16)
    fwd = jnp.dot(tile, col_v, preferred_element_type=jnp.float32)
    if with_back:
        back = lax.dot_general(
            tile, row_v, (((0,), (0,)), ((), ())), preferred_element_type=jnp.float32
        )
    else:
        back = jnp.zeros_like(fwd)
    return (fwd, back)


def local(features, start_block, counts, reach):
    rows = features.shape[0]
    nblk = counts.shape[0]
    width = start_block.shape[1]
    feat = features.shape[1]
    head = MAXREACH * BLOCK
    gamma = 1.0 / feat
    valid = (
        (jnp.arange(BLOCK, dtype=jnp.int32)[None, :] < counts[:, None])
        .astype(jnp.bfloat16)
        .reshape(rows)
    )
    next_x, next_m = shifted((features[:head], valid[:head]), "frames", -1)
    ext_x = jnp.concatenate([features, next_x], 0)
    ext_m = jnp.concatenate([valid, next_m], 0).astype(jnp.float32)
    total = rows * lax.axis_size("frames")
    vec = start_block
    basis = jnp.zeros((rows, width), jnp.float32)
    proj = jnp.zeros((width, width), jnp.float32)
    for step in range(ITERS):
        next_v = shifted(vec[:head], "frames", -1)
        ext_v = jnp.concatenate([vec, next_v], 0)

        def row_step(blk, acc):
            rstart = blk * BLOCK
            row_x = lax.dynamic_slice_in_dim(ext_x, rstart, BLOCK, 0)
            row_m = lax.dynamic_slice_in_dim(ext_m, rstart, BLOCK, 0)
            row_v = lax.dynamic_slice_in_dim(ext_v, rstart, BLOCK, 0)
            for off in range(MAXREACH + 1):
                cstart = rstart + off * BLOCK
                col_x = lax.dynamic_slice_in_dim(ext_x, cstart, BLOCK, 0)
                col_m = lax.dynamic_slice_in_dim(ext_m, cstart, BLOCK, 0)
                col_v = lax.dynamic_slice_in_dim(ext_v, cstart, BLOCK, 0)
                active = off <= reach[blk]
                fwd, back = contribute(
                    row_x, row_m, row_v, col_x, col_m, col_v, gamma, active, off > 0
                )
                acc = lax.dynamic_update_slice_in_dim(
                    acc, lax.dynamic_slice_in_dim(acc, rstart, BLOCK, 0) + fwd, rstart, 0
                )
                if off > 0:
                    acc = lax.dynamic_update_slice_in_dim(
                        acc, lax.dynamic_slice_in_dim(acc, cstart, BLOCK, 0) + back, cstart, 0
                    )
            return acc

        acc = lax.fori_loop(0, nblk, row_step, jnp.zeros((rows + head, width), jnp.float32))
        returned = shifted(acc[rows:], "frames", 1)
        image = acc[:rows] + jnp.pad(returned, ((0, rows - head), (0, 0)))
        gram = lax.dot_general(
            image,
            image,
            (((0,), (0,)), ((), ())),
            precision=lax.Precision.HIGHEST,
            preferred_element_type=jnp.float32,
        )
        proj = lax.dot_general(
            vec.astype(jnp.float32),
            image,
            (((0,), (0,)), ((), ())),
            precision=lax.Precision.HIGHEST,
            preferred_element_type=jnp.float32,
        )
        gram, proj = lax.psum((gram, proj), "frames")
        low = jnp.linalg.cholesky(gram)
        basis = jax.scipy.linalg.solve_triangular(low, image.T, lower=True).T * math.sqrt(total)
        vec = basis.astype(jnp.bfloat16)
    return (basis, proj / (total * BLOCK))


def solution(mesh):
    in_specs = (
        P(("streams", "frames"), None),
        P(("streams", "frames"), None),
        P(("streams", "frames")),
        P(("streams", "frames")),
    )
    out_specs = (P(("streams", "frames"), None), P("streams", None))
    return jax.shard_map(local, mesh=mesh, in_specs=in_specs, out_specs=out_specs, check_vma=False)
```

profile of v0, /device:TPU:0, one launch (start us, length us, event | category | flops | bytes accessed | tf_op | source)
XLA Modules:
  0.0 529.0 jit_solution(18149164961068238503)
XLA Ops:
  8.0 1.3 collective-permute-start.1
  9.3 1.9 slice.47
  11.2 1.4 collective-permute-start
  13.6 1.3 collective-permute-start.2
  15.0 3.4 collective-permute-done.2
  18.4 1.9 pad_maximum_fusion
  21.5 28.9 %while.45 = (s32[]{:T(128)}, f32[3072,128]{1,0:T(8,128)S(1)}, bf16[3072,256]{1,0:T(8,128)(2,1)S(1)}, f32[3072]{0:T(1024)S(1)}, s32[4]{0:T(128)S(1)}, /*index=5*/...) while((s32[]{:T(128)}, f32[3072,128]{1,0:T(8,128)S(1)}, ...), condition=%wide.region_4.5_spmd, body=%wide.region_0.4_spmd.sunk | while | flops 745994752 | bytes 11710913 | solution.py:88
  23.3 1.6 fusion.300
  30.5 1.6 fusion.300
  37.8 1.6 fusion.300
  45.0 1.6 fusion.300
  50.5 10.4 %collective-permute-start.3 = (f32[1024,128]{1,0:T(8,128)S(1)}, f32[1024,128]{1,0:T(8,128)S(1)}, u32[]{:S(2)}, u32[]{:S(2)}) collective-permute-start(f32[1024,128]{1,0:T(8,128)S(1)} %slice.53), channel_id=1, source_target_pairs={{0,1},{1,2},{2,3},{3,4},{4,5},{5,6},{6,7},{7,8},{8,9},{9,10},{10,1... | collective-permute-start | bytes 1572872 | tf_op jit(solution)/shard_map/ppermute | solution.py:16
  60.9 1.5 collective-permute-done.3
  63.2 2.5 fusion.178
  65.9 92.6 %all-reduce.8.cloned.1.call-done = f32[128,128]{0,1:T(8,128)} async-done(((f32[128,128]{0,1:T(8,128)}), f32[128,128]{0,1:T(8,128)}) %all-reduce.8.cloned.1.call-update) | async-done | bytes 65552 | tf_op jit(solution)/shard_map/psum | solution.py:105
  160.3 11.7 %cholesky.59 = f32[128,128]{1,0:T(8,128)S(1)} custom-call(f32[128,128]{1,0:T(8,128)S(1)} %fusion.190), custom_call_target="Cholesky" | custom-call | tf_op jit(solution)/shard_map/jit(cholesky)/cholesky | solution.py:106
  173.3 9.8 %custom-call.7 = f32[1,128,128]{1,2,0:T(8,128)S(1)} custom-call(f32[1,128,128]{2,1,0:T(8,128)S(1)} %fusion.182), custom_call_target="InvertDiagBlocksLowerTriangular" | custom-call | tf_op jit(solution)/shard_map/jit(_solve_triangular)/triangular_solve | solution.py:107
  183.2 2.1 fusion.174
  186.1 1.3 collective-permute-start.4
  187.4 2.1 collective-permute-done.4
  191.9 28.9 %while.46 = (s32[]{:T(128)}, f32[3072,128]{1,0:T(8,128)S(1)}, bf16[3072,256]{1,0:T(8,128)(2,1)S(1)}, f32[3072]{0:T(1024)S(1)}, s32[4]{0:T(128)S(1)}, /*index=5*/...) while((s32[]{:T(128)}, f32[3072,128]{1,0:T(8,128)S(1)}, ...), condition=%wide.region_12.0_spmd, body=%wide.region_8.14_spmd.sunk | while | flops 745994752 | bytes 11710913 | solution.py:88
  193.7 1.6 fusion.322
  200.9 1.6 fusion.322
  208.1 1.6 fusion.322
  215.4 1.6 fusion.322
  220.9 6.7 %collective-permute-start.5 = (f32[1024,128]{1,0:T(8,128)S(1)}, f32[1024,128]{1,0:T(8,128)S(1)}, u32[]{:S(2)}, u32[]{:S(2)}) collective-permute-start(f32[1024,128]{1,0:T(8,128)S(1)} %slice.56), channel_id=1, source_target_pairs={{0,1},{1,2},{2,3},{3,4},{4,5},{5,6},{6,7},{7,8},{8,9},{9,10},{10,1... | collective-permute-start | bytes 1572872 | tf_op jit(solution)/shard_map/ppermute | solution.py:16
  227.6 1.3 collective-permute-done.5
  229.6 2.5 fusion.179
  232.2 92.1 %all-reduce.10.cloned.1.call-done = f32[128,128]{0,1:T(8,128)} async-done(((f32[128,128]{0,1:T(8,128)}), f32[128,128]{0,1:T(8,128)}) %all-reduce.10.cloned.1.call-update) | async-done | bytes 65552 | tf_op jit(solution)/shard_map/psum | solution.py:105
  326.1 11.7 %cholesky.70 = f32[128,128]{1,0:T(8,128)S(1)} custom-call(f32[128,128]{1,0:T(8,128)S(1)} %fusion.188), custom_call_target="Cholesky" | custom-call | tf_op jit(solution)/shard_map/jit(cholesky)/cholesky | solution.py:106
  339.2 9.8 %custom-call.8 = f32[1,128,128]{1,2,0:T(8,128)S(1)} custom-call(f32[1,128,128]{2,1,0:T(8,128)S(1)} %fusion.183), custom_call_target="InvertDiagBlocksLowerTriangular" | custom-call | tf_op jit(solution)/shard_map/jit(_solve_triangular)/triangular_solve | solution.py:107
  349.0 2.1 fusion.173
  351.9 1.3 collective-permute-start.6
  353.2 2.1 collective-permute-done.6
  357.7 28.9 %while.47 = (s32[]{:T(128)}, f32[3072,128]{1,0:T(8,128)S(1)}, bf16[3072,256]{1,0:T(8,128)(2,1)S(1)}, f32[3072]{0:T(1024)S(1)}, s32[4]{0:T(128)S(1)}, /*index=5*/...) while((s32[]{:T(128)}, f32[3072,128]{1,0:T(8,128)S(1)}, ...), condition=%wide.region_18.21_spmd, body=%wide.region_14.20_spmd.sunk | while | flops 745994752 | bytes 11710913 | solution.py:88
  359.5 1.6 fusion.344
  366.7 1.6 fusion.344
  373.9 1.6 fusion.344
  381.2 1.6 fusion.344
  386.7 6.8 %collective-permute-start.7 = (f32[1024,128]{1,0:T(8,128)S(1)}, f32[1024,128]{1,0:T(8,128)S(1)}, u32[]{:S(2)}, u32[]{:S(2)}) collective-permute-start(f32[1024,128]{1,0:T(8,128)S(1)} %slice.59), channel_id=1, source_target_pairs={{0,1},{1,2},{2,3},{3,4},{4,5},{5,6},{6,7},{7,8},{8,9},{9,10},{10,1... | collective-permute-start | bytes 1572872 | tf_op jit(solution)/shard_map/ppermute | solution.py:16
  393.5 1.2 collective-permute-done.7
  394.7 2.4 fusion.180
  397.0 2.5 fusion.181
  399.5 94.8 %all-reduce.12.cloned.1.call-done = (f32[128,128]{0,1:T(8,128)}, f32[128,128]{1,0:T(8,128)}) async-done(((f32[128,128]{0,1:T(8,128)}, f32[128,128]{1,0:T(8,128)}), (f32[128,128]{0,1:T(8,128)}, f32[128,128]{1,0:T(8,128)})) %all-reduce.12.cloned.1.call-update) | async-done | bytes 131088 | tf_op jit(solution)/shard_map/psum | solution.py:105
  495.3 1.5 fusion.186
  496.8 11.7 %cholesky.81 = f32[128,128]{1,0:T(8,128)S(1)} custom-call(f32[128,128]{1,0:T(8,128)S(1)} %get-tuple-element.544), custom_call_target="Cholesky" | custom-call | tf_op jit(solution)/shard_map/jit(cholesky)/cholesky | solution.py:106
  509.9 9.8 %custom-call.9 = f32[1,128,128]{1,2,0:T(8,128)S(1)} custom-call(f32[1,128,128]{2,1,0:T(8,128)S(1)} %fusion.184), custom_call_target="InvertDiagBlocksLowerTriangular" | custom-call | tf_op jit(solution)/shard_map/jit(_solve_triangular)/triangular_solve | solution.py:107
  520.8 1.3 copy.14
  (189 shorter events, 61.9 us)
Async XLA Ops:
  7.2 7.7 %copy-start.5 = (bf16[2048,256]{1,0:T(8,128)(2,1)S(1)}, bf16[2048,256]{1,0:T(8,128)(2,1)}, u32[]{:S(2)}) copy-start(bf16[2048,256]{1,0:T(8,128)(2,1)} %param.13) | copy-start | bytes 3145732
  7.2 151.3 %all-reduce.8.cloned.1.call-start = ((), (), s32[]{:S(2)}) async-start(), calls=%async_computation | async-start | bytes 131072 | tf_op jit(solution)/shard_map/psum | solution.py:105
  8.0 7.0 %collective-permute-start.1 = (bf16[1024]{0:T(1024)(128)(2,1)S(1)}, bf16[1024]{0:T(1024)(128)(2,1)S(1)}, u32[]{:S(2)}, u32[]{:S(2)}) collective-permute-start(bf16[1024]{0:T(1024)(128)(2,1)S(1)} %bitcast.114), channel_id=1, source_target_pairs={{1,0},{2,1},{3,2},{4,3},{5,4},{6,5},{7,6},{8,7},{9,8},{10,9},{11,1... | collective-permute-start | bytes 6152 | tf_op jit(solution)/shard_map/ppermute | solution.py:16
  11.2 7.2 %copy-start.8 = (bf16[2048,128]{1,0:T(8,128)(2,1)S(1)}, bf16[2048,128]{1,0:T(8,128)(2,1)}, u32[]{:S(2)}) copy-start(bf16[2048,128]{1,0:T(8,128)(2,1)} %param.14) | copy-start | bytes 1572868
  11.2 9.1 %collective-permute-start = (bf16[1024,256]{1,0:T(8,128)(2,1)}, bf16[1024,256]{1,0:T(8,128)(2,1)}, u32[]{:S(2)}, u32[]{:S(2)}) collective-permute-start(bf16[1024,256]{1,0:T(8,128)(2,1)} %slice.47), channel_id=1, source_target_pairs={{1,0},{2,1},{3,2},{4,3},{5,4},{6,5},{7,6},{8,7},{9,8},{10,9},{11,1... | collective-permute-start | bytes 1572872 | tf_op jit(solution)/shard_map/ppermute | solution.py:16
  13.6 4.8 collective-permute-start.2
  20.3 1.2 copy-start.9
  24.9 1.3 copy-start.1
  32.1 1.3 copy-start.1
  39.3 1.3 copy-start.1
  46.6 1.3 copy-start.1
  50.5 11.9 %collective-permute-start.3 = (f32[1024,128]{1,0:T(8,128)S(1)}, f32[1024,128]{1,0:T(8,128)S(1)}, u32[]{:S(2)}, u32[]{:S(2)}) collective-permute-start(f32[1024,128]{1,0:T(8,128)S(1)} %slice.53), channel_id=1, source_target_pairs={{0,1},{1,2},{2,3},{3,4},{4,5},{5,6},{6,7},{7,8},{8,9},{9,10},{10,1... | collective-permute-start | bytes 1572872 | tf_op jit(solution)/shard_map/ppermute | solution.py:16
  62.4 0.8 copy-start.6
  65.7 258.6 %all-reduce.10.cloned.1.call-start = ((), (), s32[]{:S(2)}) async-start(), calls=%async_computation.1 | async-start | bytes 131072 | tf_op jit(solution)/shard_map/psum | solution.py:105
  185.3 0.8 copy-start.4
  186.1 3.4 collective-permute-start.4
  195.2 1.3 copy-start.2
  202.5 1.3 copy-start.2
  209.7 1.3 copy-start.2
  216.9 1.3 copy-start.2
  220.9 8.0 %collective-permute-start.5 = (f32[1024,128]{1,0:T(8,128)S(1)}, f32[1024,128]{1,0:T(8,128)S(1)}, u32[]{:S(2)}, u32[]{:S(2)}) collective-permute-start(f32[1024,128]{1,0:T(8,128)S(1)} %slice.56), channel_id=1, source_target_pairs={{0,1},{1,2},{2,3},{3,4},{4,5},{5,6},{6,7},{7,8},{8,9},{9,10},{10,1... | collective-permute-start | bytes 1572872 | tf_op jit(solution)/shard_map/ppermute | solution.py:16
  228.9 0.8 copy-start.7
  232.1 262.2 %all-reduce.12.cloned.1.call-start = ((), (), s32[]{:S(2)}) async-start(), calls=%async_computation.2 | async-start | bytes 262144 | tf_op jit(solution)/shard_map/psum | solution.py:105
  351.1 0.8 copy-start.3
  351.9 3.4 collective-permute-start.6
  361.0 1.3 copy-start
  368.3 1.3 copy-start
  375.5 1.3 copy-start
  382.7 1.3 copy-start
  386.7 8.0 %collective-permute-start.7 = (f32[1024,128]{1,0:T(8,128)S(1)}, f32[1024,128]{1,0:T(8,128)S(1)}, u32[]{:S(2)}, u32[]{:S(2)}) collective-permute-start(f32[1024,128]{1,0:T(8,128)S(1)} %slice.59), channel_id=1, source_target_pairs={{0,1},{1,2},{2,3},{3,4},{4,5},{5,6},{6,7},{7,8},{8,9},{9,10},{10,1... | collective-permute-start | bytes 1572872 | tf_op jit(solution)/shard_map/ppermute | solution.py:16
Sparse Core Ops, SparseCore 0:
  65.8 92.6 all-reduce.7
  232.3 92.0 all-reduce.9
  399.7 94.6 all-reduce.11
where the time goes:
time: 536 us; the launch traced here: 529 us
  waiting for transfers between devices  291 us (54%)
  other arithmetic  80.2 us (15%)
  matrix products  62.2 us (12%)
  starting transfers between devices  30.8 us (6%)
  loops' own time  27 us (5%)
  local copies, waits for them, and re-layouts  23.1 us (4%)
  between operations  14.5 us (3%)
    psum x3, waiting for transfers between devices, local(): gram, proj = lax.psum((gram, proj), 'frames')  280 us
    another operation x9, other arithmetic, local(): low = jnp.linalg.cholesky(gram)  37.2 us
    another operation x6, other arithmetic, local(): jax.scipy.linalg.solve_triangular(low, image.T, lower=True)  31.4 us
    ppermute x8, starting transfers between devices, shifted(): lax.ppermute(value, axis, [(source, source + steps) for source in range(i...  30.5 us
    another operation x3, loops' own time, local(): lax.fori_loop(0, nblk, row_step, jnp.zeros((rows + head, width), jnp.floa...  27 us
    dot_general x36, matrix products, contribute(): fwd = jnp.dot(tile, col_v, preferred_element_type=jnp.float32)  26.1 us
    dot_general x24, matrix products, affinity(): lax.dot_general(row_x, col_x, (((1,), (1,)), ((), ())), preferred_element...  12.6 us
    ppermute x8, waiting for transfers between devices, shifted(): lax.ppermute(value, axis, [(source, source + steps) for source in range(i...  11.7 us
  transfers between devices with their start and end apart: 11, of which 9 were waited for; matrix products, arithmetic and copies ran while one was open for 1% of the time, Pallas kernels for 0%

commit v1 on v0

v1 whole, which is shorter than its diff:
```python
import functools
import math

import jax
import jax.numpy as jnp
from jax import lax
from jax.experimental import pallas as pl
from jax.experimental.pallas import tpu as pltpu
from jax.sharding import PartitionSpec as P

BLOCK = 512
MAXREACH = 2
ITERS = 3
OFFS = 2 * MAXREACH + 1
LANE = 128
SUB = 8
ROWS = 128
OFF = -1e30
HI = lax.Precision.HIGHEST
F32 = jnp.float32
BF16 = jnp.bfloat16
NN = (((1,), (0,)), ((), ()))
NT = (((1,), (1,)), ((), ()))
TN = (((0,), (0,)), ((), ()))


def dot(left, right, dims, precision=None):
    return lax.dot_general(left, right, dims, precision=precision, preferred_element_type=F32)


def inverse_factor(gram):
    width = gram.shape[0]
    count = width // SUB
    mat = [gram[SUB * i : SUB * (i + 1), :] for i in range(count)]
    sub = lax.broadcasted_iota(jnp.int32, (SUB, width), 0)
    lane = lax.broadcasted_iota(jnp.int32, (SUB, width), 1)

    def down(value, k):
        return jnp.broadcast_to(value[k : k + 1, :], (SUB, width))

    def across(value, c):
        return jnp.broadcast_to(value[:, c : c + 1], (SUB, width))

    for b in range(count):
        first = SUB * b
        inside = (lane >= first) & (lane < first + SUB)
        cols = [[across(mat[i], first + k) for k in range(SUB)] for i in range(b, count)]
        panel = jnp.where(inside, jnp.where(lane == first + sub, 1.0, 0.0), mat[b])
        for i in range(b + 1, count):
            mat[i] = jnp.where(inside, 0.0, mat[i])
        for k in range(SUB):
            scale = lax.rsqrt(down(cols[0][k], k))
            for col in cols:
                col[k] = col[k] * scale
            for m in range(k + 1, SUB):
                factor = down(cols[0][k], m)
                for col in cols:
                    col[m] = col[m] - col[k] * factor
            row = down(panel, k) * scale
            panel = jnp.where(
                sub == k, row, jnp.where(sub > k, panel - cols[0][k] * row, panel)
            )
            for i in range(b + 1, count):
                mat[i] = mat[i] - cols[i - b][k] * row
        mat[b] = jnp.where(lane < first + SUB, panel, 0.0)
    return jnp.concatenate(mat, 0)


def kernel(
    n, axis, counts, reach, x_hbm, v_hbm, basis_ref, ray_ref,
    xext, vext, meta, oper, image, cbias, rbias, part, parts_in, chunk, whole, pbuf,
    lsem, hsend, hrecv, rsend, rrecv, gsend, grecv, csend, crecv,
):
    nblk = counts.shape[0]
    width = vext.shape[-1]
    feat = xext.shape[-1]
    total = n * nblk * BLOCK
    ext = nblk + 2 * MAXREACH
    size = parts_in.shape[1]
    groups = n // size
    me = lax.axis_index(axis)
    rank = lax.rem(me, size)
    base = me - rank
    has_left = me > 0
    has_right = me < n - 1

    def peer(step):
        return base + lax.rem(rank + step, size)

    def group_peer(step):
        return lax.rem(me + step * size, n)

    own_x = pltpu.make_async_copy(x_hbm, xext.at[pl.ds(MAXREACH, nblk)], lsem.at[0])
    own_v = pltpu.make_async_copy(v_hbm, vext.at[0, pl.ds(MAXREACH, nblk)], lsem.at[1])
    own_x.start()
    own_v.start()

    for j in range(nblk):
        meta[1, j : j + 1, :] = jnp.full((1, LANE), counts[j]).astype(F32)
        meta[1, nblk + j : nblk + j + 1, :] = jnp.full((1, LANE), reach[j]).astype(F32)

    @pl.when(jnp.logical_not(has_left))
    def _():
        meta[0] = jnp.zeros_like(meta[0])
        xext[0:MAXREACH] = jnp.zeros((MAXREACH, BLOCK, feat), BF16)
        for s in range(ITERS):
            vext[s, 0:MAXREACH] = jnp.zeros((MAXREACH, BLOCK, width), BF16)

    @pl.when(jnp.logical_not(has_right))
    def _():
        meta[2] = jnp.zeros_like(meta[2])
        xext[ext - MAXREACH : ext] = jnp.zeros((MAXREACH, BLOCK, feat), BF16)
        for s in range(ITERS):
            vext[s, ext - MAXREACH : ext] = jnp.zeros((MAXREACH, BLOCK, width), BF16)

    barrier = pltpu.get_barrier_semaphore()
    for step in range(1, size):
        pl.semaphore_signal(barrier, inc=1, device_id={axis: peer(step)}, device_id_type=pl.DeviceIdType.MESH)
    for step in range(1, groups):
        pl.semaphore_signal(barrier, inc=1, device_id={axis: group_peer(step)}, device_id_type=pl.DeviceIdType.MESH)

    @pl.when(has_left)
    def _():
        pl.semaphore_signal(barrier, inc=1, device_id={axis: me - 1}, device_id_type=pl.DeviceIdType.MESH)

    @pl.when(has_right)
    def _():
        pl.semaphore_signal(barrier, inc=1, device_id={axis: me + 1}, device_id_type=pl.DeviceIdType.MESH)

    pl.semaphore_wait(
        barrier, size - 1 + groups - 1 + has_left.astype(jnp.int32) + has_right.astype(jnp.int32)
    )

    def copy(src, dst, sem_row, sem_col, target):
        return pltpu.make_async_remote_copy(
            src_ref=src, dst_ref=dst, send_sem=hsend.at[sem_row, sem_col],
            recv_sem=hrecv.at[sem_row, sem_col], device_id={axis: target},
            device_id_type=pl.DeviceIdType.MESH,
        )

    def halo(row, source, dest, j, left):
        if left:
            return copy(source(j), dest(ext - MAXREACH + j), row, MAXREACH + j, me - 1)
        return copy(source(nblk - MAXREACH + j), dest(j), row, j, me + 1)

    def x_halo(j, left):
        return halo(ITERS, lambda b: x_hbm.at[b], lambda b: xext.at[b], j, left)

    def v_halo(s, j, left):
        if s == 0:
            return halo(s, lambda b: v_hbm.at[b], lambda b: vext.at[s, b], j, left)
        return halo(s, lambda b: vext.at[s, MAXREACH + b], lambda b: vext.at[s, b], j, left)

    def m_halo(left):
        if left:
            return copy(meta.at[1], meta.at[2], ITERS + 1, 1, me - 1)
        return copy(meta.at[1], meta.at[0], ITERS + 1, 0, me + 1)

    near = [(j, True) for j in range(MAXREACH)], [(j, False) for j in reversed(range(MAXREACH))]

    def each(left, action):
        @pl.when(has_left if left else has_right)
        def _():
            action()

    def comes(left, action):
        @pl.when(has_right if left else has_left)
        def _():
            action()

    for left in (True, False):
        def start(left=left):
            m_halo(left).start()
            for j, side in near[0 if left else 1]:
                x_halo(j, side).start()
            for j, side in near[0 if left else 1]:
                v_halo(0, j, side).start()
        each(left, start)

    gamma2 = math.log2(math.e) / feat

    def col_bias(e):
        xe = xext[e].astype(F32)
        norm = dot(jnp.ones((SUB, feat), F32), xe * xe, NT, HI)
        side, j = (0, nblk - MAXREACH + e) if e < MAXREACH else (
            (1, e - MAXREACH) if e < nblk + MAXREACH else (2, e - nblk - MAXREACH))
        held = jnp.concatenate([meta[side, j : j + 1, :]] * (BLOCK // LANE), 1)
        at = lax.broadcasted_iota(jnp.int32, (1, BLOCK), 1).astype(F32)
        cbias[e : e + 1, :] = jnp.where(at < held, -gamma2 * norm[0:1, :], OFF)

    def row_bias(i):
        xe = xext[MAXREACH + i].astype(F32)
        norm = jnp.sum(xe * xe, 1, keepdims=True)
        at = lax.broadcasted_iota(jnp.int32, (BLOCK, 1), 0).astype(F32)
        rbias[i] = jnp.where(at < meta[1, i : i + 1, 0:1], -gamma2 * norm, OFF)

    def tiles(i, offsets):
        bias = []
        for o in offsets:
            d = o - MAXREACH
            if d >= 0:
                far = meta[1, nblk + i : nblk + i + 1, :]
            else:
                b = i + d
                far = meta[1, nblk + b : nblk + b + 1, :] if b >= 0 else meta[0, 2 * nblk + b : 2 * nblk + b + 1, :]
            far = jnp.concatenate([far] * (BLOCK // LANE), 1)
            bias.append(jnp.where(far >= float(abs(d)), cbias[i + o : i + o + 1, :], OFF))

        def rows_step(r, carry):
            at = pl.multiple_of(r * ROWS, ROWS)
            rows = xext[MAXREACH + i, pl.ds(at, ROWS), :]
            left = rbias[i, pl.ds(at, ROWS), :]
            for o, right in zip(offsets, bias):
                inner = dot(rows, xext[i + o], NT)
                oper[i, pl.ds(at, ROWS), o * BLOCK : (o + 1) * BLOCK] = jnp.exp2(
                    inner * (2.0 * gamma2) + (left + right)
                ).astype(BF16)
            return carry

        lax.fori_loop(0, BLOCK // ROWS, rows_step, 0)

    own = [[o for o in range(OFFS) if MAXREACH <= i + o < nblk + MAXREACH] for i in range(nblk)]
    edge = [[o for o in range(OFFS) if o not in own[i]] for i in range(nblk)]

    own_x.wait()
    for j in range(nblk):
        col_bias(MAXREACH + j)
        row_bias(j)
    for i in range(nblk):
        tiles(i, own[i])
    for left in (True, False):
        def arrive(left=left):
            m_halo(left).wait_recv()
            for j, side in near[0 if left else 1]:
                x_halo(j, side).wait_recv()
        comes(left, arrive)
    for e in list(range(MAXREACH)) + list(range(ext - MAXREACH, ext)):
        col_bias(e)
    for i in range(nblk):
        tiles(i, edge[i])
    own_v.wait()

    def product(s, i, offsets):
        first, last = offsets[0], offsets[-1] + 1
        vec = vext[s, i + first : i + last].reshape((last - first) * BLOCK, width)
        return dot(oper[i, :, first * BLOCK : last * BLOCK], vec, NN)

    def reduce_start(s, which):
        for step in range(1, size):
            q = lax.rem(rank + step, size)
            pltpu.make_async_remote_copy(
                src_ref=part.at[s, which, q], dst_ref=parts_in.at[2 * s + which, rank],
                send_sem=rsend.at[2 * s + which, step], recv_sem=rrecv.at[2 * s + which, rank],
                device_id={axis: base + q}, device_id_type=pl.DeviceIdType.MESH,
            ).start()

    def reduce_rest(s, which):
        row = 2 * s + which

        def incoming(q):
            return pltpu.make_async_remote_copy(
                src_ref=part.at[s, which, q], dst_ref=parts_in.at[row, q],
                send_sem=rsend.at[row, 0], recv_sem=rrecv.at[row, q],
                device_id={axis: base + q}, device_id_type=pl.DeviceIdType.MESH,
            )

        total_chunk = part[s, which, rank]
        for step in range(1, size):
            q = lax.rem(rank + step, size)
            incoming(q).wait_recv()
            total_chunk = total_chunk + parts_in[row, q]
        if groups > 1:
            me_group = me // size
            chunk[row, me_group] = total_chunk

            def cross(step):
                return pltpu.make_async_remote_copy(
                    src_ref=chunk.at[row, me_group], dst_ref=chunk.at[row, me_group],
                    send_sem=csend.at[row, step], recv_sem=crecv.at[row, step],
                    device_id={axis: group_peer(step)}, device_id_type=pl.DeviceIdType.MESH,
                )

            for step in range(1, groups):
                cross(step).start()
            for step in range(1, groups):
                cross(step).wait_recv()
            total_chunk = chunk[row, 0]
            for g in range(1, groups):
                total_chunk = total_chunk + chunk[row, g]
            for step in range(1, groups):
                cross(step).wait_send()
        whole[row, rank] = total_chunk

        def gather(step, q):
            return pltpu.make_async_remote_copy(
                src_ref=whole.at[row, rank], dst_ref=whole.at[row, rank],
                send_sem=gsend.at[row, step], recv_sem=grecv.at[row, rank],
                device_id={axis: base + q}, device_id_type=pl.DeviceIdType.MESH,
            )

        for step in range(1, size):
            gather(step, lax.rem(rank + step, size)).start()

    def reduce_done(s, which):
        row = 2 * s + which
        for step in range(1, size):
            q = lax.rem(rank + step, size)
            pltpu.make_async_remote_copy(
                src_ref=whole.at[row, q], dst_ref=whole.at[row, q],
                send_sem=gsend.at[row, step], recv_sem=grecv.at[row, q],
                device_id={axis: base + q}, device_id_type=pl.DeviceIdType.MESH,
            ).wait_recv()
        return jnp.concatenate([whole[row, q] for q in range(size)], 0)

    def reduce_clear(s, which):
        row = 2 * s + which
        for step in range(1, size):
            q = lax.rem(rank + step, size)
            pltpu.make_async_remote_copy(
                src_ref=part.at[s, which, q], dst_ref=parts_in.at[row, rank],
                send_sem=rsend.at[row, step], recv_sem=rrecv.at[row, rank],
                device_id={axis: base + q}, device_id_type=pl.DeviceIdType.MESH,
            ).wait_send()
            pltpu.make_async_remote_copy(
                src_ref=whole.at[row, rank], dst_ref=whole.at[row, rank],
                send_sem=gsend.at[row, step], recv_sem=grecv.at[row, rank],
                device_id={axis: base + q}, device_id_type=pl.DeviceIdType.MESH,
            ).wait_send()

    def split(value):
        return value.reshape(size, width // size, width)

    order = [j for pair in zip(range(nblk), reversed(range(nblk))) for j in pair][:nblk]
    for s in range(ITERS):
        for i in range(nblk):
            image[i] = product(s, i, own[i])
        for left in (True, False):
            def arrive(left=left, s=s):
                for j, side in near[0 if left else 1]:
                    v_halo(s, j, side).wait_recv()
            comes(left, arrive)
        gram = None
        for i in range(nblk):
            if edge[i]:
                runs = [[o for o in edge[i] if i + o < MAXREACH], [o for o in edge[i] if i + o >= MAXREACH]]
                value = image[i]
                for run in runs:
                    if run:
                        value = value + product(s, i, run)
                image[i] = value
            else:
                value = image[i]
            term = dot(value, value, TN, HI)
            gram = term if gram is None else gram + term
        part[s, 0] = split(gram)
        reduce_start(s, 0)
        if s == ITERS - 1:
            proj = None
            for i in range(nblk):
                term = dot(vext[s, MAXREACH + i].astype(F32), image[i], TN, HI)
                proj = term if proj is None else proj + term
            part[s, 1] = split(proj)
            reduce_start(s, 1)
        reduce_rest(s, 0)
        if s == ITERS - 1:
            reduce_rest(s, 1)
        gram = reduce_done(s, 0)
        inv = inverse_factor(gram) * math.sqrt(total)
        for i in order:
            basis = dot(image[i], inv, NT, HI)
            if s == ITERS - 1:
                basis_ref[i] = basis
                continue
            vext[s + 1, MAXREACH + i] = basis.astype(BF16)
            if i < MAXREACH:
                each(True, lambda s=s, i=i: v_halo(s + 1, i, True).start())
            if i >= nblk - MAXREACH:
                each(False, lambda s=s, i=i: v_halo(s + 1, i - nblk + MAXREACH, False).start())
    ray_ref[...] = reduce_done(ITERS - 1, 1) * (1.0 / (total * BLOCK))

    for s in range(ITERS):
        reduce_clear(s, 0)
    reduce_clear(ITERS - 1, 1)
    for left in (True, False):
        def finish(left=left):
            m_halo(left).wait_send()
            for j, side in near[0 if left else 1]:
                x_halo(j, side).wait_send()
                for s in range(ITERS):
                    v_halo(s, j, side).wait_send()
        each(left, finish)


def local(axis, features, start_block, counts, reach):
    n = lax.axis_size(axis)
    nblk = counts.shape[0]
    rows, feat = features.shape
    width = start_block.shape[1]
    ext = nblk + 2 * MAXREACH
    size = min(n, width // SUB)
    groups = n // size
    rung = width // size
    sems = pltpu.SemaphoreType.DMA
    any_spec = pl.BlockSpec(memory_space=pl.ANY)
    smem = pl.BlockSpec(memory_space=pltpu.SMEM)
    vmem = pl.BlockSpec(memory_space=pltpu.VMEM)
    rounds = 2 * ITERS
    basis, ray = pl.pallas_call(
        functools.partial(kernel, n, axis),
        out_shape=(
            jax.ShapeDtypeStruct((nblk, BLOCK, width), F32),
            jax.ShapeDtypeStruct((width, width), F32),
        ),
        in_specs=[smem, smem, any_spec, any_spec],
        out_specs=(vmem, vmem),
        scratch_shapes=[
            pltpu.VMEM((ext, BLOCK, feat), BF16),
            pltpu.VMEM((ITERS, ext, BLOCK, width), BF16),
            pltpu.VMEM((3, 2 * nblk, LANE), F32),
            pltpu.VMEM((nblk, BLOCK, OFFS * BLOCK), BF16),
            pltpu.VMEM((nblk, BLOCK, width), F32),
            pltpu.VMEM((ext, BLOCK), F32),
            pltpu.VMEM((nblk, BLOCK, 1), F32),
            pltpu.VMEM((ITERS, 2, size, rung, width), F32),
            pltpu.VMEM((rounds, size, rung, width), F32),
            pltpu.VMEM((rounds, groups, rung, width), F32),
            pltpu.VMEM((rounds, size, rung, width), F32),
            pltpu.VMEM((SUB, LANE), F32),
            sems((2,)),
            sems((ITERS + 2, 2 * MAXREACH)),
            sems((ITERS + 2, 2 * MAXREACH)),
            sems((rounds, size)),
            sems((rounds, size)),
            sems((rounds, size)),
            sems((rounds, size)),
            sems((rounds, groups)),
            sems((rounds, groups)),
        ],
        compiler_params=pltpu.CompilerParams(
            collective_id=0, has_side_effects=True, vmem_limit_bytes=48 * 1024 * 1024
        ),
    )(counts, reach, features.reshape(nblk, BLOCK, feat), start_block.reshape(nblk, BLOCK, width))
    return basis.reshape(rows, width), ray


def solution(mesh):
    in_specs = (
        P(("streams", "frames"), None),
        P(("streams", "frames"), None),
        P(("streams", "frames")),
        P(("streams", "frames")),
    )
    out_specs = (P(("streams", "frames"), None), P("streams", None))
    return jax.shard_map(
        functools.partial(local, "frames"), mesh=mesh, in_specs=in_specs, out_specs=out_specs, check_vma=False
    )
```

time: 536 us -> 103 us (0.19); the launches traced: 529 us -> 103 us
  waiting for transfers between devices: 291 us -> 0 us
  Pallas kernels: 0 us -> 97.8 us
  other arithmetic: 80.2 us -> 0 us
  matrix products: 62.2 us -> 0 us
  starting transfers between devices: 30.8 us -> 0 us
  loops' own time: 27 us -> 0 us
  local copies, waits for them, and re-layouts: 23.1 us -> 4.52 us
  between operations: 14.5 us -> 0.66 us
    psum x3 -> x0, waiting for transfers between devices: 280 us -> none  [local(): gram, proj = lax.psum((gram, proj), 'frames')]
    pallas_call x0 -> x1, Pallas kernels: none -> 97.8 us  [local(): pl.pallas_call(functools.partial(kernel, n, axis), out_shape=(jax.ShapeDt...]
    another operation x15 -> x0, other arithmetic: 68.6 us -> none  [the longest x9 37.2 us: local(): low = jnp.linalg.cholesky(gram)]
    dot_general x88 -> x0, matrix products: 56.9 us -> none  [the longest x36 26.1 us: contribute(): fwd = jnp.dot(tile, col_v, preferred_element_type=jnp.float32)]
    ppermute x8 -> x0, starting transfers between devices: 30.5 us -> none  [shifted(): lax.ppermute(value, axis, [(source, source + steps) for source in range(i...]
    another operation x3 -> x0, loops' own time: 27 us -> none  [local(): lax.fori_loop(0, nblk, row_step, jnp.zeros((rows + head, width), jnp.floa...]
    ppermute x8 -> x0, waiting for transfers between devices: 11.7 us -> none  [shifted(): lax.ppermute(value, axis, [(source, source + steps) for source in range(i...]
    dynamic_slice x24 -> x0, local copies, waits for them, and re-layouts: 9.01 us -> none  [the longest x12 7.96 us: row_step(): active = off <= reach[blk]]
  transfers between devices with their start and end apart: 11 -> 0, of which waited for: 9 -> 0; matrix products, arithmetic and copies ran while one was open for 1% -> 0% of each run, Pallas kernels for 0% -> 0%
where the time goes in v1:
time: 103 us
  Pallas kernels  97.8 us (95%)
  local copies, waits for them, and re-layouts  4.52 us (4%)
    pallas_call x1, Pallas kernels, local(): pl.pallas_call(functools.partial(kernel, n, axis), out_shape=(jax.ShapeDt...  97.8 us
    unnamed x10, local copies, waits for them, and re-layouts  4.52 us

profile of v1, /device:TPU:0, one launch (start us, length us, event | category | flops | bytes accessed | tf_op | source)
XLA Modules:
  0.0 103.0 jit_solution(6085520479102403122)
XLA Ops:
  0.6 0.0 copy-start.2
  0.6 0.0 copy-start.3
  0.7 0.6 copy-done.2
  1.3 0.0 copy-done.3
  1.3 0.0 copy-start
  1.3 1.2 %copy-done = bf16[2048,256]{1,0:T(8,128)(2,1)S(1)} copy-done((bf16[2048,256]{1,0:T(8,128)(2,1)S(1)}, bf16[2048,256]{1,0:T(8,128)(2,1)}, u32[]{:S(2)}) %copy-start) | copy-done | bytes 1048600
  2.5 0.0 copy-start.1
  2.5 1.0 %copy-done.1 = bf16[2048,128]{1,0:T(8,128)(2,1)S(1)} copy-done((bf16[2048,128]{1,0:T(8,128)(2,1)S(1)}, bf16[2048,128]{1,0:T(8,128)(2,1)}, u32[]{:S(2)}) %copy-start.1) | copy-done | bytes 524312
  3.6 97.8 %shard_map.59 = (f32[4,512,128]{2,1,0:T(8,128)S(1)}, f32[128,128]{1,0:T(8,128)S(1)}) custom-call(s32[4]{0:T(128)S(1)} %copy-done.2, s32[4]{0:T(128)S(1)} %copy-done.3, bf16[4,512,256]{2,1,0:T(8,128)(2,1)S(1)} %bitcast.3, bf16[4,512,128]{2,1,0:T(8,128)(2,1)S(1)} %bitcast.5), custom_call_target="tpu_custom_call" | custom-call | tf_op jit(solution)/shard_map/pallas_call | solution.py:408
  101.4 1.0 copy.8
  102.3 0.6 copy.9
Async XLA Ops:
  0.6 0.7 copy-start.2
  0.6 0.7 copy-start.3
  1.3 1.2 %copy-start = (bf16[2048,256]{1,0:T(8,128)(2,1)S(1)}, bf16[2048,256]{1,0:T(8,128)(2,1)}, u32[]{:S(2)}) copy-start(bf16[2048,256]{1,0:T(8,128)(2,1)} %param.4) | copy-start | bytes 3145732
  2.5 1.0 %copy-start.1 = (bf16[2048,128]{1,0:T(8,128)(2,1)S(1)}, bf16[2048,128]{1,0:T(8,128)(2,1)}, u32[]{:S(2)}) copy-start(bf16[2048,128]{1,0:T(8,128)(2,1)} %param.5) | copy-start | bytes 1572868

commit v2 on v1

--- a/solution.py
+++ b/solution.py
@@ -103,15 +103,17 @@
     def _():
         meta[0] = jnp.zeros_like(meta[0])
         xext[0:MAXREACH] = jnp.zeros((MAXREACH, BLOCK, feat), BF16)
-        for s in range(ITERS):
-            vext[s, 0:MAXREACH] = jnp.zeros((MAXREACH, BLOCK, width), BF16)
+        for s in range(ITERS - 1):
+            image[s, 0:MAXREACH] = jnp.zeros((MAXREACH, BLOCK, width), F32)
+        vext[0, 0:MAXREACH] = jnp.zeros((MAXREACH, BLOCK, width), BF16)
 
     @pl.when(jnp.logical_not(has_right))
     def _():
         meta[2] = jnp.zeros_like(meta[2])
         xext[ext - MAXREACH : ext] = jnp.zeros((MAXREACH, BLOCK, feat), BF16)
-        for s in range(ITERS):
-            vext[s, ext - MAXREACH : ext] = jnp.zeros((MAXREACH, BLOCK, width), BF16)
+        for s in range(ITERS - 1):
+            image[s, ext - MAXREACH : ext] = jnp.zeros((MAXREACH, BLOCK, width), F32)
+        vext[0, ext - MAXREACH : ext] = jnp.zeros((MAXREACH, BLOCK, width), BF16)
 
     barrier = pltpu.get_barrier_semaphore()
     for step in range(1, size):
@@ -146,10 +148,11 @@
     def x_halo(j, left):
         return halo(ITERS, lambda b: x_hbm.at[b], lambda b: xext.at[b], j, left)
 
-    def v_halo(s, j, left):
-        if s == 0:
-            return halo(s, lambda b: v_hbm.at[b], lambda b: vext.at[s, b], j, left)
-        return halo(s, lambda b: vext.at[s, MAXREACH + b], lambda b: vext.at[s, b], j, left)
+    def v_halo(j, left):
+        return halo(ITERS - 1, lambda b: v_hbm.at[b], lambda b: vext.at[0, b], j, left)
+
+    def i_halo(s, j, left):
+        return halo(s, lambda b: image.at[s, MAXREACH + b], lambda b: image.at[s, b], j, left)
 
     def m_halo(left):
         if left:
@@ -174,7 +177,7 @@
             for j, side in near[0 if left else 1]:
                 x_halo(j, side).start()
             for j, side in near[0 if left else 1]:
-                v_halo(0, j, side).start()
+                v_halo(j, side).start()
         each(left, start)
 
     gamma2 = math.log2(math.e) / feat
@@ -245,30 +248,25 @@
         vec = vext[s, i + first : i + last].reshape((last - first) * BLOCK, width)
         return dot(oper[i, :, first * BLOCK : last * BLOCK], vec, NN)
 
+    def remote(src, dst, send, recv, q):
+        return pltpu.make_async_remote_copy(
+            src_ref=src, dst_ref=dst, send_sem=send, recv_sem=recv,
+            device_id={axis: base + q}, device_id_type=pl.DeviceIdType.MESH,
+        )
+
     def reduce_start(s, which):
+        row = 2 * s + which
         for step in range(1, size):
             q = lax.rem(rank + step, size)
-            pltpu.make_async_remote_copy(
-                src_ref=part.at[s, which, q], dst_ref=parts_in.at[2 * s + which, rank],
-                send_sem=rsend.at[2 * s + which, step], recv_sem=rrecv.at[2 * s + which, rank],
-                device_id={axis: base + q}, device_id_type=pl.DeviceIdType.MESH,
-            ).start()
+            remote(part.at[s, which, q], parts_in.at[row, step - 1], rsend.at[row], rrecv.at[row], q).start()
 
     def reduce_rest(s, which):
         row = 2 * s + which
-
-        def incoming(q):
-            return pltpu.make_async_remote_copy(
-                src_ref=part.at[s, which, q], dst_ref=parts_in.at[row, q],
-                send_sem=rsend.at[row, 0], recv_sem=rrecv.at[row, q],
-                device_id={axis: base + q}, device_id_type=pl.DeviceIdType.MESH,
-            )
-
+        slots = parts_in.at[row, pl.ds(0, size - 1)]
+        remote(slots, slots, rsend.at[row], rrecv.at[row], rank).wait_recv()
         total_chunk = part[s, which, rank]
         for step in range(1, size):
-            q = lax.rem(rank + step, size)
-            incoming(q).wait_recv()
-            total_chunk = total_chunk + parts_in[row, q]
+            total_chunk = total_chunk + parts_in[row, step - 1]
         if groups > 1:
             me_group = me // size
             chunk[row, me_group] = total_chunk
@@ -290,66 +288,47 @@
             for step in range(1, groups):
                 cross(step).wait_send()
         whole[row, rank] = total_chunk
-
-        def gather(step, q):
-            return pltpu.make_async_remote_copy(
-                src_ref=whole.at[row, rank], dst_ref=whole.at[row, rank],
-                send_sem=gsend.at[row, step], recv_sem=grecv.at[row, rank],
-                device_id={axis: base + q}, device_id_type=pl.DeviceIdType.MESH,
-            )
-
         for step in range(1, size):
-            gather(step, lax.rem(rank + step, size)).start()
+            q = lax.rem(rank + step, size)
+            remote(whole.at[row, rank], whole.at[row, rank], gsend.at[row], grecv.at[row], q).start()
 
     def reduce_done(s, which):
         row = 2 * s + which
-        for step in range(1, size):
-            q = lax.rem(rank + step, size)
-            pltpu.make_async_remote_copy(
-                src_ref=whole.at[row, q], dst_ref=whole.at[row, q],
-                send_sem=gsend.at[row, step], recv_sem=grecv.at[row, q],
-                device_id={axis: base + q}, device_id_type=pl.DeviceIdType.MESH,
-            ).wait_recv()
+        slots = parts_in.at[row, pl.ds(0, size - 1)]
+        remote(slots, slots, gsend.at[row], grecv.at[row], rank).wait_recv()
         return jnp.concatenate([whole[row, q] for q in range(size)], 0)
 
     def reduce_clear(s, which):
         row = 2 * s + which
-        for step in range(1, size):
-            q = lax.rem(rank + step, size)
-            pltpu.make_async_remote_copy(
-                src_ref=part.at[s, which, q], dst_ref=parts_in.at[row, rank],
-                send_sem=rsend.at[row, step], recv_sem=rrecv.at[row, rank],
-                device_id={axis: base + q}, device_id_type=pl.DeviceIdType.MESH,
-            ).wait_send()
-            pltpu.make_async_remote_copy(
-                src_ref=whole.at[row, rank], dst_ref=whole.at[row, rank],
-                send_sem=gsend.at[row, step], recv_sem=grecv.at[row, rank],
-                device_id={axis: base + q}, device_id_type=pl.DeviceIdType.MESH,
-            ).wait_send()
+        slots = parts_in.at[row, pl.ds(0, size - 1)]
+        remote(slots, slots, rsend.at[row], rrecv.at[row], rank).wait_send()
+        remote(slots, slots, gsend.at[row], grecv.at[row], rank).wait_send()
 
     def split(value):
         return value.reshape(size, width // size, width)
 
     order = [j for pair in zip(range(nblk), reversed(range(nblk))) for j in pair][:nblk]
+    inner = list(range(MAXREACH, nblk + MAXREACH))
     for s in range(ITERS):
         for i in range(nblk):
-            image[i] = product(s, i, own[i])
-        for left in (True, False):
-            def arrive(left=left, s=s):
-                for j, side in near[0 if left else 1]:
-                    v_halo(s, j, side).wait_recv()
-            comes(left, arrive)
+            image[s, MAXREACH + i] = product(s, i, own[i])
+        if s == 0:
+            for left in (True, False):
+                def arrive(left=left):
+                    for j, side in near[0 if left else 1]:
+                        v_halo(j, side).wait_recv()
+                comes(left, arrive)
+        for i in order:
+            runs = [[o for o in edge[i] if i + o < MAXREACH], [o for o in edge[i] if i + o >= MAXREACH]]
+            value = image[s, MAXREACH + i]
+            for run in runs:
+                if run:
+                    value = value + product(s, i, run)
+            if edge[i]:
+                image[s, MAXREACH + i] = value
         gram = None
         for i in range(nblk):
-            if edge[i]:
-                runs = [[o for o in edge[i] if i + o < MAXREACH], [o for o in edge[i] if i + o >= MAXREACH]]
-                value = image[i]
-                for run in runs:
-                    if run:
-                        value = value + product(s, i, run)
-                image[i] = value
-            else:
-                value = image[i]
+            value = image[s, MAXREACH + i]
             term = dot(value, value, TN, HI)
             gram = term if gram is None else gram + term
         part[s, 0] = split(gram)
@@ -357,25 +336,36 @@
         if s == ITERS - 1:
             proj = None
             for i in range(nblk):
-                term = dot(vext[s, MAXREACH + i].astype(F32), image[i], TN, HI)
+                term = dot(vext[s, MAXREACH + i].astype(F32), image[s, MAXREACH + i], TN, HI)
                 proj = term if proj is None else proj + term
             part[s, 1] = split(proj)
             reduce_start(s, 1)
         reduce_rest(s, 0)
         if s == ITERS - 1:
             reduce_rest(s, 1)
+        if s < ITERS - 1:
+            for left in (True, False):
+                def send(left=left, s=s):
+                    for j, side in near[0 if left else 1]:
+                        i_halo(s, j, side).start()
+                each(left, send)
         gram = reduce_done(s, 0)
         inv = inverse_factor(gram) * math.sqrt(total)
-        for i in order:
-            basis = dot(image[i], inv, NT, HI)
+        for e in inner:
+            basis = dot(image[s, e], inv, NT, HI)
             if s == ITERS - 1:
-                basis_ref[i] = basis
-                continue
-            vext[s + 1, MAXREACH + i] = basis.astype(BF16)
-            if i < MAXREACH:
-                each(True, lambda s=s, i=i: v_halo(s + 1, i, True).start())
-            if i >= nblk - MAXREACH:
-                each(False, lambda s=s, i=i: v_halo(s + 1, i - nblk + MAXREACH, False).start())
+                basis_ref[e - MAXREACH] = basis
+            else:
+                vext[s + 1, e] = basis.astype(BF16)
+        if s < ITERS - 1:
+            for left in (True, False):
+                def arrive(left=left, s=s):
+                    for j, side in near[0 if left else 1]:
+                        i_halo(s, j, side).wait_recv()
+                comes(left, arrive)
+            for e in range(ext):
+                if e not in inner:
+                    vext[s + 1, e] = dot(image[s, e], inv, NT, HI).astype(BF16)
     ray_ref[...] = reduce_done(ITERS - 1, 1) * (1.0 / (total * BLOCK))
 
     for s in range(ITERS):
@@ -386,8 +376,9 @@
             m_halo(left).wait_send()
             for j, side in near[0 if left else 1]:
                 x_halo(j, side).wait_send()
-                for s in range(ITERS):
-                    v_halo(s, j, side).wait_send()
+                v_halo(j, side).wait_send()
+                for s in range(ITERS - 1):
+                    i_halo(s, j, side).wait_send()
         each(left, finish)
 
 
@@ -418,7 +409,7 @@
             pltpu.VMEM((ITERS, ext, BLOCK, width), BF16),
             pltpu.VMEM((3, 2 * nblk, LANE), F32),
             pltpu.VMEM((nblk, BLOCK, OFFS * BLOCK), BF16),
-            pltpu.VMEM((nblk, BLOCK, width), F32),
+            pltpu.VMEM((ITERS, ext, BLOCK, width), F32),
             pltpu.VMEM((ext, BLOCK), F32),
             pltpu.VMEM((nblk, BLOCK, 1), F32),
             pltpu.VMEM((ITERS, 2, size, rung, width), F32),
@@ -429,15 +420,15 @@
             sems((2,)),
             sems((ITERS + 2, 2 * MAXREACH)),
             sems((ITERS + 2, 2 * MAXREACH)),
-            sems((rounds, size)),
-            sems((rounds, size)),
-            sems((rounds, size)),
-            sems((rounds, size)),
+            sems((rounds,)),
+            sems((rounds,)),
+            sems((rounds,)),
+            sems((rounds,)),
             sems((rounds, groups)),
             sems((rounds, groups)),
         ],
         compiler_params=pltpu.CompilerParams(
-            collective_id=0, has_side_effects=True, vmem_limit_bytes=48 * 1024 * 1024
+            collective_id=0, has_side_effects=True, vmem_limit_bytes=60 * 1024 * 1024
         ),
     )(counts, reach, features.reshape(nblk, BLOCK, feat), start_block.reshape(nblk, BLOCK, width))
     return basis.reshape(rows, width), ray

time: 103 us -> 96.1 us (0.933)
  Pallas kernels: 97.8 us -> 92.3 us
  local copies, waits for them, and re-layouts: 4.52 us -> 2.93 us
    pallas_call x1, Pallas kernels: 97.8 us -> 92.3 us  [local(): pl.pallas_call(functools.partial(kernel, n, axis), out_shape=(jax.ShapeDt...]
    unnamed x10 -> x4, local copies, waits for them, and re-layouts: 4.52 us -> 2.93 us
where the time goes in v2:
time: 96.1 us; the launch traced here: 95.9 us
  Pallas kernels  92.3 us (96%)
  local copies, waits for them, and re-layouts  2.93 us (3%)
    pallas_call x1, Pallas kernels, local(): pl.pallas_call(functools.partial(kernel, n, axis), out_shape=(jax.ShapeDt...  92.3 us
    unnamed x4, local copies, waits for them, and re-layouts  2.93 us

profile of v2, /device:TPU:0, one launch (start us, length us, event | category | flops | bytes accessed | tf_op | source)
XLA Modules:
  0.0 95.9 jit_solution(17991381588204240829)
XLA Ops:
  0.6 92.3 %shard_map.59 = (f32[4,512,128]{2,1,0:T(8,128)}, f32[128,128]{1,0:T(8,128)}) custom-call(s32[4]{0:T(128)} %counts.1, s32[4]{0:T(128)} %reach.1, bf16[4,512,256]{2,1,0:T(8,128)(2,1)} %bitcast.3, bf16[4,512,128]{2,1,0:T(8,128)(2,1)} %bitcast.5), custom_call_target="tpu_custom_call" | custom-call | tf_op jit(solution)/shard_map/pallas_call | solution.py:399
  93.0 0.0 copy-start
  93.0 2.3 %copy.8 = f32[2048,128]{1,0:T(8,128)} copy(f32[2048,128]{1,0:T(8,128)} %bitcast.4) | data formatting | bytes 2097152
  95.3 0.0 copy-done
  95.3 0.6 copy.9
Async XLA Ops:
  93.0 2.3 %copy-start = (f32[128,128]{1,0:T(8,128)S(1)}, f32[128,128]{1,0:T(8,128)}, u32[]{:S(2)}) copy-start(f32[128,128]{1,0:T(8,128)} %get-tuple-element.9) | copy-start | bytes 196612
